TPU v7x, 32 devices: a whole 2x2x4 slice. The times are simulated.
32 devices in a mesh: member: 2 (over y), comp: 2 (over core), tile: 4 (over z), sub: 2 (over x).
Axes of the slice: x: 2, y: 2, z: 4, core: 2. Of those that a mesh axis runs over, the one named last changes fastest.
Arguments:
- tracers: float32 [2, 6, 32, 32, 256], P('comp', 'member', None, 'tile', 'sub'), parts along dimension 1, may hold values from -6 to 6
- couple: float32 [2, 64, 32, 256], P('comp', 'member', 'tile', 'sub'), parts along dimension 1, may hold values from 0.3 to 10
- send_cell: int32 [2, 8, 8, 128], P('comp', ('tile', 'sub')), may hold values from 0 to 1023
- recv_pos: int32 [2, 8, 16384], P('comp', ('tile', 'sub')), may hold values from 0 to 1023, as said below
- row_count: int32 [8], P(('tile', 'sub')), may hold values from 1024 to 16384, as said below
- sea_mask: int32 [8, 16384], P(('tile', 'sub')), may hold values 0 or 1
- exch_coef: float32 [6, 8, 16384], P('member', ('tile', 'sub')), parts along dimension 0, may hold values from 0.3 to 3
- margin_area: float32 [2, 8, 16384], P('comp', ('tile', 'sub')), may hold values from 0.2 to 1
Outputs:
- updated: float32 [2, 6, 32, 32, 256], P('comp', 'member', None, 'tile', 'sub'), parts along dimension 1
There are 2 independent parts, one for each index of `member`. A program takes and returns all parts, laid end to end along the dimension named above; an argument that names none is the same for every part. Nothing has to cross between parts.
Inputs may be any that keep to these rules, and one draw needn't show every extreme that they name: Rows of owner o from row_count[o] on are padding; in every draw some owner holds 16384 live rows. recv_pos[c, o, r] = s * 128 + k names entry k of the list that device s of component c sends to owner o.
All inputs are finite; a program needn't handle non-finite values. No bound on the sum of `sea_mask` on one device may be relied on, other than what follows from the above.
Results may differ from a plain program's by a relative error of at most 0.00002.
Values sent between devices are 32-bit elements; how exact they have to be, the bound alone decides.
A program may use at most 64 MiB of HBM per device.

v0:
```python
import jax
import jax.numpy as jnp
from jax import lax
from jax.sharding import PartitionSpec as P

SMOOTH_RATE = 0.2


def extended(array, sides, width):
    for axis, dim in sides:
        count, length = (lax.axis_size(axis), array.shape[dim])
        up = [(i, (i + 1) % count) for i in range(count - 1)]
        down = [(j, i) for i, j in up]
        last = lax.slice_in_dim(array, length - width, length, axis=dim)
        first = lax.slice_in_dim(array, 0, width, axis=dim)
        before = lax.ppermute(last, axis, up)
        after = lax.ppermute(first, axis, down)
        array = jnp.concatenate([before, array, after], axis=dim)
    return array


def from_partner(value, axis, stride):
    mask = 2**stride
    pairs = [(source, source ^ mask) for source in range(lax.axis_size(axis))]
    return lax.ppermute(value, axis, pairs)


def laplace_inner(padded):
    beside_all = (
        padded[..., 2:, 1:-1]
        + padded[..., :-2, 1:-1]
        + padded[..., 1:-1, 2:]
        + padded[..., 1:-1, :-2]
    )
    return beside_all - 4.0 * padded[..., 1:-1, 1:-1]


def smooth_rim(field):
    padded = extended(field, (("tile", 2), ("sub", 3)), 1)
    return field + SMOOTH_RATE * laplace_inner(padded)


def per_device(tracers, couple, send_cell, recv_pos, row_count, sea_mask, exch_coef, margin_area):
    fields = tracers[0]
    coupling = couple[0]
    nvar, nlev, rows_a, cols_b = fields.shape
    smooth_once = smooth_rim(fields)
    smooth_twice = smooth_rim(smooth_once)
    zeros_plane = jnp.zeros_like(coupling[0])
    offsets = []
    factors = []
    for level in range(nlev):
        couple_above = coupling[level]
        couple_below = coupling[level + 1] if level + 1 < nlev else zeros_plane
        if level == 0:
            pivot = 1.0 + couple_above + couple_below
            offset_now = fields[:, 0] / pivot[None]
        else:
            pivot = 1.0 + couple_above + couple_below - couple_above * factors[-1]
            offset_now = (fields[:, level] + couple_above[None] * offsets[-1]) / pivot[None]
        offsets.append(offset_now)
        factors.append(couple_below / pivot)
    surface_e = offsets[-1]
    surface_f = 1.0 / pivot
    surface = jnp.concatenate([surface_e, surface_f[None]], axis=0)
    table = surface.reshape(nvar + 1, rows_a * cols_b).T
    owners = send_cell.shape[2]
    slot_count = send_cell.shape[3]
    lists = send_cell[0, 0]
    outgoing = jnp.take(table, lists, axis=0).reshape(owners, slot_count * (nvar + 1))
    incoming = lax.all_to_all(outgoing, ("tile", "sub"), split_axis=0, concat_axis=0, tiled=True)
    received = incoming.reshape(owners * slot_count, nvar + 1)
    positions = recv_pos[0, 0]
    row_total = positions.shape[0]
    own_rows = jnp.take(received, positions, axis=0).T
    other_rows = from_partner(own_rows, "comp", 0)
    coef = exch_coef[:, 0]
    live = ((jnp.arange(row_total, dtype=jnp.int32) < row_count[0]) & (sea_mask[0] == 1)).astype(
        jnp.float32
    )
    weight = live * margin_area[0, 0]
    flux = (
        coef
        * (other_rows[:nvar] - own_rows[:nvar])
        / (1.0 + coef * (own_rows[nvar:] + other_rows[nvar:]))
    )
    flux = flux * weight[None]
    slot_sums = jax.ops.segment_sum(flux.T, positions, num_segments=owners * slot_count)
    slot_sums = slot_sums.reshape(owners, slot_count * nvar)
    returned = lax.all_to_all(slot_sums, ("tile", "sub"), split_axis=0, concat_axis=0, tiled=True)
    cell_flux = jax.ops.segment_sum(
        returned.reshape(owners * slot_count, nvar), lists.reshape(-1), num_segments=rows_a * cols_b
    )
    cell_flux = cell_flux.T.reshape(nvar, rows_a, cols_b)
    column = surface_e + surface_f[None] * cell_flux
    stacked = [column]
    for level in range(nlev - 2, -1, -1):
        column = offsets[level] + factors[level][None] * column
        stacked.append(column)
    vertical = jnp.stack(stacked[::-1], axis=1)
    updated = vertical + (smooth_twice - fields)
    return updated[None]


def solution(mesh):
    placed = (
        P("comp", "member", None, "tile", "sub"),
        P("comp", "member", "tile", "sub"),
        P("comp", ("tile", "sub"), None, None),
        P("comp", ("tile", "sub"), None),
        P(("tile", "sub")),
        P(("tile", "sub"), None),
        P("member", ("tile", "sub"), None),
        P("comp", ("tile", "sub"), None),
    )
    return jax.shard_map(
        per_device,
        mesh=mesh,
        in_specs=placed,
        out_specs=P("comp", "member", None, "tile", "sub"),
        check_vma=False,
    )
```

profile of v0, /device:TPU:0, one launch (start us, length us, event | category | flops | bytes accessed | tf_op | source)
XLA Modules:
  0.0 239.7 jit_solution(9058169392339581085)
XLA Ops:
  0.0 1.3 fusion.84
  1.3 1.5 slice_bitcast_fusion.91
  2.8 1.5 slice_bitcast_fusion.83
  4.2 1.5 slice_bitcast_fusion.79
  5.7 1.5 slice_bitcast_fusion.33
  7.2 0.9 slice_bitcast_fusion.30
  8.1 0.9 slice_bitcast_fusion.29
  9.0 0.7 bitcast_add_fusion.30
  9.7 0.9 slice_add_fusion.1
  12.8 2.8 %gather_fusion = f32[1024,4]{1,0:T(8,128)S(1)} fusion(f32[1024,4]{1,0:T(8,128)S(1)} %bitcast.837, s32[1024]{0:T(1024)S(1)} %fusion.117), kind=kCustom, calls=%fused_computation | custom fusion | bytes 36864 | tf_op jit(solution)/shard_map/jit(_take)/gather | solution.py:70
  15.6 0.9 copy.455
  17.5 7.3 %all-to-all-start = ((f32[8,1,512]{2,1,0:T(1,128)}), f32[8,1,512]{2,1,0:T(1,128)S(1)}, u32[]{:S(2)}, u32[]{:S(2)}) async-start(f32[8,1,512]{2,1,0:T(1,128)} %copy.456), calls=%async_computation | async-start | bytes 32768 | tf_op jit(solution)/shard_map/all_to_all | solution.py:71
  24.8 1.3 collective-permute-start.1
  26.1 4.5 %collective-permute-start.2 = (f32[3,32,1,128]{3,2,1,0:T(1,128)S(1)}, f32[3,32,1,128]{3,2,1,0:T(1,128)S(1)}, u32[]{:S(2)}, u32[]{:S(2)}) collective-permute-start(f32[3,32,1,128]{3,2,1,0:T(1,128)S(1)} %get-tuple-element.122), channel_id=1, source_target_pairs={{0,2},{2,4},{4,6},{1,3},{3,5},{5,7},{8,10},{10,12},{12,14},{9,11},... | collective-permute-start | bytes 147464 | tf_op jit(solution)/shard_map/ppermute | solution.py:16
  36.3 1.3 collective-permute-start.3
  37.9 4.5 %collective-permute-start.4 = (f32[3,32,10,1]{1,3,2,0:T(1,128)S(1)}, f32[3,32,10,1]{1,3,2,0:T(1,128)S(1)}, u32[]{:S(2)}, u32[]{:S(2)}) collective-permute-start(f32[3,32,10,1]{1,3,2,0:T(1,128)S(1)} %copy.463), channel_id=1, source_target_pairs={{0,1},{2,3},{4,5},{6,7},{8,9},{10,11},{12,13},{14,15},{16,17},{18,... | collective-permute-start | bytes 11528 | tf_op jit(solution)/shard_map/ppermute | solution.py:16
  43.7 54.8 %gather_fusion.1 = f32[16384,4]{1,0:T(8,128)} fusion(f32[1024,4]{1,0:T(8,128)S(1)} %reshape.13368, s32[16384]{0:T(1024)S(1)} %broadcast_clamp_fusion), kind=kCustom, calls=%fused_computation.1 | custom fusion | bytes 589824 | tf_op jit(solution)/shard_map/jit(_take)/gather | solution.py:75
  98.6 5.5 %copy.457 = f32[16384,4]{0,1:T(4,128)S(1)} copy(f32[16384,4]{1,0:T(8,128)} %gather_fusion.1) | data formatting | bytes 524288 | tf_op jit(solution)/shard_map/jit(_take)/gather | solution.py:75
  105.6 1.3 collective-permute-start.5
  106.9 4.6 %collective-permute-start.6 = (f32[3,32,1,128]{3,2,1,0:T(1,128)S(1)}, f32[3,32,1,128]{3,2,1,0:T(1,128)S(1)}, u32[]{:S(2)}, u32[]{:S(2)}) collective-permute-start(f32[3,32,1,128]{3,2,1,0:T(1,128)S(1)} %get-tuple-element.120), channel_id=1, source_target_pairs={{0,2},{2,4},{4,6},{1,3},{3,5},{5,7},{8,10},{10,12},{12,14},{9,11},... | collective-permute-start | bytes 147464 | tf_op jit(solution)/shard_map/ppermute | solution.py:16
  111.7 1.5 collective-permute-done.6
  113.9 1.3 collective-permute-start.7
  115.5 4.5 %collective-permute-start.8 = (f32[3,32,10,1]{1,3,2,0:T(1,128)S(1)}, f32[3,32,10,1]{1,3,2,0:T(1,128)S(1)}, u32[]{:S(2)}, u32[]{:S(2)}) collective-permute-start(f32[3,32,10,1]{1,3,2,0:T(1,128)S(1)} %copy.467), channel_id=1, source_target_pairs={{0,1},{2,3},{4,5},{6,7},{8,9},{10,11},{12,13},{14,15},{16,17},{18,... | collective-permute-start | bytes 11528 | tf_op jit(solution)/shard_map/ppermute | solution.py:16
  120.2 1.2 multiply_bitcast_fusion
  121.4 5.1 %copy.458 = f32[16384,3]{1,0:T(8,128)} copy(f32[16384,3]{0,1:T(4,128)S(1)} %multiply_bitcast_fusion) | data formatting | bytes 393216 | tf_op jit(solution)/shard_map/transpose | solution.py:88
  126.4 87.7 %scatter_custom_fusion = f32[1024,3]{1,0:T(8,128)S(1)} fusion(s32[16384]{0:T(1024)S(1)} %bitcast.850, f32[16384,3]{1,0:T(8,128)} %copy.458, f32[]{:T(128)} %constant.20.clone.1), kind=kCustom, calls=%fused_computation.47 | custom fusion | flops 49152 | bytes 12800 | tf_op jit(solution)/shard_map/scatter-add | solution.py:88
  214.2 1.0 all_to_all.13
  215.2 6.0 %all-to-all-start.1 = ((f32[8,1,384]{2,1,0:T(1,128)}), f32[8,1,384]{2,1,0:T(1,128)S(1)}, u32[]{:S(2)}, u32[]{:S(2)}) async-start(f32[8,1,384]{2,1,0:T(1,128)} %all_to_all.13), calls=%async_computation.1 | async-start | bytes 24576 | tf_op jit(solution)/shard_map/all_to_all | solution.py:90
  222.7 5.0 %all-to-all-done.1 = f32[8,1,384]{2,1,0:T(1,128)S(1)} async-done(((f32[8,1,384]{2,1,0:T(1,128)}), f32[8,1,384]{2,1,0:T(1,128)S(1)}, u32[]{:S(2)}, u32[]{:S(2)}) %all-to-all-start.1) | async-done | bytes 12320 | tf_op jit(solution)/shard_map/all_to_all | solution.py:90
  228.1 6.3 %scatter_custom_fusion.1 = f32[1024,3]{1,0:T(8,128)S(1)} fusion(s32[1024]{0:T(1024)} %bitcast.884, f32[1024,3]{1,0:T(8,128)S(1)} %reshape.13399, f32[]{:T(128)} %constant.20.clone.1), kind=kCustom, calls=%fused_computation.45 | custom fusion | flops 3072 | bytes 12800 | tf_op jit(solution)/shard_map/scatter-add | solution.py:91
  234.5 1.4 constant_dynamic-update-slice_fusion.31
  238.3 1.3 fusion.6
  (163 shorter events, 16.6 us)
Async XLA Ops:
  17.5 25.6 %all-to-all-start = ((f32[8,1,512]{2,1,0:T(1,128)}), f32[8,1,512]{2,1,0:T(1,128)S(1)}, u32[]{:S(2)}, u32[]{:S(2)}) async-start(f32[8,1,512]{2,1,0:T(1,128)} %copy.456), calls=%async_computation | async-start | bytes 32768 | tf_op jit(solution)/shard_map/all_to_all | solution.py:71
  24.8 10.8 %collective-permute-start.1 = (f32[3,32,1,128]{3,2,1,0:T(1,128)S(1)}, f32[3,32,1,128]{3,2,1,0:T(1,128)S(1)}, u32[]{:S(2)}, u32[]{:S(2)}) collective-permute-start(f32[3,32,1,128]{3,2,1,0:T(1,128)S(1)} %get-tuple-element.123), channel_id=1, source_target_pairs={{2,0},{4,2},{6,4},{3,1},{5,3},{7,5},{10,8},{12,10},{14,12},{11,9},... | collective-permute-start | bytes 147464 | tf_op jit(solution)/shard_map/ppermute | solution.py:17
  26.1 9.5 %collective-permute-start.2 = (f32[3,32,1,128]{3,2,1,0:T(1,128)S(1)}, f32[3,32,1,128]{3,2,1,0:T(1,128)S(1)}, u32[]{:S(2)}, u32[]{:S(2)}) collective-permute-start(f32[3,32,1,128]{3,2,1,0:T(1,128)S(1)} %get-tuple-element.122), channel_id=1, source_target_pairs={{0,2},{2,4},{4,6},{1,3},{3,5},{5,7},{8,10},{10,12},{12,14},{9,11},... | collective-permute-start | bytes 147464 | tf_op jit(solution)/shard_map/ppermute | solution.py:16
  33.3 187.8 %copy-start.8 = (f32[8,128]{1,0:T(8,128)}, f32[8,128]{1,0:T(8,128)S(1)}, u32[]{:S(2)}) copy-start(f32[8,128]{1,0:T(8,128)S(1)} %get-tuple-element.46) | copy-start | bytes 12292
  33.3 65.1 %copy-start.9 = (f32[8,128]{1,0:T(8,128)}, f32[8,128]{1,0:T(8,128)S(1)}, u32[]{:S(2)}) copy-start(f32[8,128]{1,0:T(8,128)S(1)} %get-tuple-element.48) | copy-start | bytes 12292
  33.3 187.8 %copy-start.10 = (f32[8,128]{1,0:T(8,128)}, f32[8,128]{1,0:T(8,128)S(1)}, u32[]{:S(2)}) copy-start(f32[8,128]{1,0:T(8,128)S(1)} %get-tuple-element.49) | copy-start | bytes 12292
  33.3 65.1 %copy-start.11 = (f32[8,128]{1,0:T(8,128)}, f32[8,128]{1,0:T(8,128)S(1)}, u32[]{:S(2)}) copy-start(f32[8,128]{1,0:T(8,128)S(1)} %get-tuple-element.51) | copy-start | bytes 12292
  33.4 65.1 %copy-start.12 = (f32[8,128]{1,0:T(8,128)}, f32[8,128]{1,0:T(8,128)S(1)}, u32[]{:S(2)}) copy-start(f32[8,128]{1,0:T(8,128)S(1)} %get-tuple-element.52) | copy-start | bytes 12292
  33.4 65.1 %copy-start.13 = (f32[8,128]{1,0:T(8,128)}, f32[8,128]{1,0:T(8,128)S(1)}, u32[]{:S(2)}) copy-start(f32[8,128]{1,0:T(8,128)S(1)} %get-tuple-element.54) | copy-start | bytes 12292
  33.4 65.1 %copy-start.14 = (f32[8,128]{1,0:T(8,128)}, f32[8,128]{1,0:T(8,128)S(1)}, u32[]{:S(2)}) copy-start(f32[8,128]{1,0:T(8,128)S(1)} %get-tuple-element.55) | copy-start | bytes 12292
  33.4 65.1 %copy-start.15 = (f32[8,128]{1,0:T(8,128)}, f32[8,128]{1,0:T(8,128)S(1)}, u32[]{:S(2)}) copy-start(f32[8,128]{1,0:T(8,128)S(1)} %get-tuple-element.57) | copy-start | bytes 12292
  33.4 65.1 %copy-start.16 = (f32[8,128]{1,0:T(8,128)}, f32[8,128]{1,0:T(8,128)S(1)}, u32[]{:S(2)}) copy-start(f32[8,128]{1,0:T(8,128)S(1)} %get-tuple-element.58) | copy-start | bytes 12292
  33.5 65.0 %copy-start.17 = (f32[8,128]{1,0:T(8,128)}, f32[8,128]{1,0:T(8,128)S(1)}, u32[]{:S(2)}) copy-start(f32[8,128]{1,0:T(8,128)S(1)} %get-tuple-element.60) | copy-start | bytes 12292
  33.5 65.0 %copy-start.18 = (f32[8,128]{1,0:T(8,128)}, f32[8,128]{1,0:T(8,128)S(1)}, u32[]{:S(2)}) copy-start(f32[8,128]{1,0:T(8,128)S(1)} %get-tuple-element.61) | copy-start | bytes 12292
  33.5 65.0 %copy-start.19 = (f32[8,128]{1,0:T(8,128)}, f32[8,128]{1,0:T(8,128)S(1)}, u32[]{:S(2)}) copy-start(f32[8,128]{1,0:T(8,128)S(1)} %get-tuple-element.63) | copy-start | bytes 12292
  33.5 65.0 %copy-start.20 = (f32[8,128]{1,0:T(8,128)}, f32[8,128]{1,0:T(8,128)S(1)}, u32[]{:S(2)}) copy-start(f32[8,128]{1,0:T(8,128)S(1)} %get-tuple-element.64) | copy-start | bytes 12292
  33.5 65.0 %copy-start.21 = (f32[8,128]{1,0:T(8,128)}, f32[8,128]{1,0:T(8,128)S(1)}, u32[]{:S(2)}) copy-start(f32[8,128]{1,0:T(8,128)S(1)} %get-tuple-element.66) | copy-start | bytes 12292
  33.6 65.0 %copy-start.22 = (f32[8,128]{1,0:T(8,128)}, f32[8,128]{1,0:T(8,128)S(1)}, u32[]{:S(2)}) copy-start(f32[8,128]{1,0:T(8,128)S(1)} %get-tuple-element.67) | copy-start | bytes 12292
  33.6 187.5 %copy-start.24 = (f32[8,128]{1,0:T(8,128)}, f32[8,128]{1,0:T(8,128)S(1)}, u32[]{:S(2)}) copy-start(f32[8,128]{1,0:T(8,128)S(1)} %get-tuple-element.70) | copy-start | bytes 12292
  33.6 187.5 %copy-start.26 = (f32[8,128]{1,0:T(8,128)}, f32[8,128]{1,0:T(8,128)S(1)}, u32[]{:S(2)}) copy-start(f32[8,128]{1,0:T(8,128)S(1)} %get-tuple-element.73) | copy-start | bytes 12292
  36.3 67.8 %collective-permute-start.3 = (f32[3,32,10,1]{1,3,2,0:T(1,128)S(1)}, f32[3,32,10,1]{1,3,2,0:T(1,128)S(1)}, u32[]{:S(2)}, u32[]{:S(2)}) collective-permute-start(f32[3,32,10,1]{1,3,2,0:T(1,128)S(1)} %copy.461), channel_id=1, source_target_pairs={{1,0},{3,2},{5,4},{7,6},{9,8},{11,10},{13,12},{15,14},{17,16},{19,... | collective-permute-start | bytes 11528 | tf_op jit(solution)/shard_map/ppermute | solution.py:17
  37.9 66.6 %collective-permute-start.4 = (f32[3,32,10,1]{1,3,2,0:T(1,128)S(1)}, f32[3,32,10,1]{1,3,2,0:T(1,128)S(1)}, u32[]{:S(2)}, u32[]{:S(2)}) collective-permute-start(f32[3,32,10,1]{1,3,2,0:T(1,128)S(1)} %copy.463), channel_id=1, source_target_pairs={{0,1},{2,3},{4,5},{6,7},{8,9},{10,11},{12,13},{14,15},{16,17},{18,... | collective-permute-start | bytes 11528 | tf_op jit(solution)/shard_map/ppermute | solution.py:16
  105.6 6.1 %collective-permute-start.5 = (f32[3,32,1,128]{3,2,1,0:T(1,128)S(1)}, f32[3,32,1,128]{3,2,1,0:T(1,128)S(1)}, u32[]{:S(2)}, u32[]{:S(2)}) collective-permute-start(f32[3,32,1,128]{3,2,1,0:T(1,128)S(1)} %get-tuple-element.121), channel_id=1, source_target_pairs={{2,0},{4,2},{6,4},{3,1},{5,3},{7,5},{10,8},{12,10},{14,12},{11,9},... | collective-permute-start | bytes 147464 | tf_op jit(solution)/shard_map/ppermute | solution.py:17
  106.9 6.3 %collective-permute-start.6 = (f32[3,32,1,128]{3,2,1,0:T(1,128)S(1)}, f32[3,32,1,128]{3,2,1,0:T(1,128)S(1)}, u32[]{:S(2)}, u32[]{:S(2)}) collective-permute-start(f32[3,32,1,128]{3,2,1,0:T(1,128)S(1)} %get-tuple-element.120), channel_id=1, source_target_pairs={{0,2},{2,4},{4,6},{1,3},{3,5},{5,7},{8,10},{10,12},{12,14},{9,11},... | collective-permute-start | bytes 147464 | tf_op jit(solution)/shard_map/ppermute | solution.py:16
  111.6 109.6 %copy-start.28 = (f32[8,128]{1,0:T(8,128)S(1)}, f32[8,128]{1,0:T(8,128)}, u32[]{:S(2)}) copy-start(f32[8,128]{1,0:T(8,128)} %get-tuple-element.76) | copy-start | bytes 12292
  111.6 109.6 %copy-start.30 = (f32[8,128]{1,0:T(8,128)S(1)}, f32[8,128]{1,0:T(8,128)}, u32[]{:S(2)}) copy-start(f32[8,128]{1,0:T(8,128)} %get-tuple-element.79) | copy-start | bytes 12292
  111.6 109.6 %copy-start.32 = (f32[8,128]{1,0:T(8,128)S(1)}, f32[8,128]{1,0:T(8,128)}, u32[]{:S(2)}) copy-start(f32[8,128]{1,0:T(8,128)} %get-tuple-element.82) | copy-start | bytes 12292
  111.6 109.6 %copy-start.34 = (f32[8,128]{1,0:T(8,128)S(1)}, f32[8,128]{1,0:T(8,128)}, u32[]{:S(2)}) copy-start(f32[8,128]{1,0:T(8,128)} %get-tuple-element.39) | copy-start | bytes 12292
  111.6 8.4 %collective-permute-start = (f32[4,16384]{1,0:T(4,128)S(1)}, f32[4,16384]{1,0:T(4,128)S(1)}, u32[]{:S(2)}, u32[]{:S(2)}) collective-permute-start(f32[4,16384]{1,0:T(4,128)S(1)} %select_bitcast_fusion), channel_id=1, source_target_pairs={{0,8},{8,0},{1,9},{9,1},{2,10},{10,2},{3,11},{11,3},{4,12},{12,4},... | collective-permute-start | bytes 786440 | tf_op jit(solution)/shard_map/ppermute | solution.py:25
  113.9 107.9 %collective-permute-start.7 = (f32[3,32,10,1]{1,3,2,0:T(1,128)S(1)}, f32[3,32,10,1]{1,3,2,0:T(1,128)S(1)}, u32[]{:S(2)}, u32[]{:S(2)}) collective-permute-start(f32[3,32,10,1]{1,3,2,0:T(1,128)S(1)} %copy.465), channel_id=1, source_target_pairs={{1,0},{3,2},{5,4},{7,6},{9,8},{11,10},{13,12},{15,14},{17,16},{19,... | collective-permute-start | bytes 11528 | tf_op jit(solution)/shard_map/ppermute | solution.py:17
  115.5 106.8 %collective-permute-start.8 = (f32[3,32,10,1]{1,3,2,0:T(1,128)S(1)}, f32[3,32,10,1]{1,3,2,0:T(1,128)S(1)}, u32[]{:S(2)}, u32[]{:S(2)}) collective-permute-start(f32[3,32,10,1]{1,3,2,0:T(1,128)S(1)} %copy.467), channel_id=1, source_target_pairs={{0,1},{2,3},{4,5},{6,7},{8,9},{10,11},{12,13},{14,15},{16,17},{18,... | collective-permute-start | bytes 11528 | tf_op jit(solution)/shard_map/ppermute | solution.py:16
  215.2 12.5 %all-to-all-start.1 = ((f32[8,1,384]{2,1,0:T(1,128)}), f32[8,1,384]{2,1,0:T(1,128)S(1)}, u32[]{:S(2)}, u32[]{:S(2)}) async-start(f32[8,1,384]{2,1,0:T(1,128)} %all_to_all.13), calls=%async_computation.1 | async-start | bytes 24576 | tf_op jit(solution)/shard_map/all_to_all | solution.py:90
  (14 other events, 511.1 us)
where the time goes:
time: 241 us; the launch traced here: 240 us
  other arithmetic  112 us (46%)
  local copies, waits for them, and re-layouts  83.4 us (35%)
  starting transfers between devices  36.6 us (15%)
  waiting for transfers between devices  6.48 us (3%)
    scatter-add x1, other arithmetic, per_device(): jax.ops.segment_sum(flux.T, positions, num_segments=owners * slot_count)  87.7 us
    gather x2, local copies, waits for them, and re-layouts, per_device(): own_rows = jnp.take(received, positions, axis=0).T  60.2 us
    ppermute x4, starting transfers between devices, extended(): before = lax.ppermute(last, axis, up)  18.2 us
    all_to_all x1, starting transfers between devices, per_device(): lax.all_to_all(outgoing, ('tile', 'sub'), split_axis=0, concat_axis=0, ti...  7.27 us
    scatter-add x1, other arithmetic, per_device(): jax.ops.segment_sum(returned.reshape(owners * slot_count, nvar), lists.re...  6.27 us
    all_to_all x1, starting transfers between devices, per_device(): lax.all_to_all(slot_sums, ('tile', 'sub'), split_axis=0, concat_axis=0, t...  5.96 us
    squeeze x4, local copies, waits for them, and re-layouts, per_device(): couple_below = coupling[level + 1] if level + 1 < nlev else zeros_plane  5.88 us
    ppermute x4, starting transfers between devices, extended(): after = lax.ppermute(first, axis, down)  5.15 us
  transfers between devices with their start and end apart: 11, of which 2 were waited for; matrix products, arithmetic and copies ran while one was open for 68% of the time, Pallas kernels for 0%

commit v1 on v0

v1 whole, which is shorter than its diff:
```python
import functools
import jax
import jax.numpy as jnp
from jax import lax
from jax.experimental import pallas as pl
from jax.experimental.pallas import tpu as pltpu
from jax.sharding import PartitionSpec as P

SMOOTH_RATE = 0.2
LANES = 128
SUBS = 8
MESH = pl.DeviceIdType.MESH
F32 = jnp.float32
BF16 = jnp.bfloat16


def lane_gather(table, index):
    return jnp.take_along_axis(table, index, axis=1, mode="promise_in_bounds")


def row_of(value, row, rows):
    return jnp.broadcast_to(value[row : row + 1], (rows, value.shape[1]))


def one_hot(low_row):
    spread = jnp.broadcast_to(low_row.astype(F32), (16, LANES)).astype(BF16)
    base = lax.broadcasted_iota(jnp.int32, (16, LANES), 0)
    one, zero = (jnp.full((16, LANES), value, BF16) for value in (1.0, 0.0))
    return jnp.concatenate(
        [
            jnp.where((base + 16 * k).astype(F32).astype(BF16) == spread, one, zero)
            for k in range(LANES // 16)
        ],
        axis=0,
    )


def contract_lanes(a, b):
    return lax.dot_general(a, b, (((1,), (1,)), ((), ())), preferred_element_type=F32)


def kernel(
    n_tile, n_sub, nvar, nlev,
    tr, couple, send_cell, pos, row_count, sea, coef, area,
    out,
    off, fac, once, dif, tab_out, tab_in, tabs, posb, areab, wgt, acc, ret_out, ret_in,
    row_s, row_r, col_s, col_r, cells,
    part_sem, halo_send, halo_recv, list_sem,
):
    owners = n_tile * n_sub
    groups = owners // SUBS
    tiles = nvar * nlev
    slab = tiles // SUBS
    half = pos.shape[0] // 2
    devices = 2 * owners
    comp, tile, sub = lax.axis_index("comp"), lax.axis_index("tile"), lax.axis_index("sub")
    me_owner = tile * n_sub + sub
    me = comp * owners + me_owner

    def place(index):
        owner = index % owners
        return {"comp": index // owners, "tile": owner // n_sub, "sub": owner % n_sub}

    barrier = pltpu.get_barrier_semaphore()

    def greet(step, carry):
        pl.semaphore_signal(
            barrier, inc=1, device_id=place((me + step) % devices), device_id_type=MESH
        )
        return carry

    lax.fori_loop(1, devices, greet, 0)

    factor = None
    offset = [None] * nvar
    for level in range(nlev):
        above = couple[level]
        below = couple[level + 1] if level + 1 < nlev else jnp.zeros_like(above)
        pivot = 1.0 + above + below
        if level > 0:
            pivot = pivot - above * factor
        inverse = 1.0 / pivot
        for var in range(nvar):
            right = tr[var * nlev + level]
            if level > 0:
                right = right + above * offset[var]
            offset[var] = right * inverse
            off[var * nlev + level] = offset[var]
        factor = below * inverse
        fac[level] = factor
    surface = offset + [inverse]

    def make_lists(group, carry):
        start = pl.multiple_of(group * SUBS, SUBS)
        cell = send_cell[pl.ds(start, SUBS), :]
        low, high = cell & (LANES - 1), cell >> 7
        for var in range(nvar + 1):
            value = jnp.zeros((SUBS, LANES), F32)
            for a in range(SUBS):
                found = lane_gather(row_of(surface[var], a, SUBS), low)
                value = jnp.where(high == a, found, value)
            for o in range(SUBS):
                tab_out[start + o, var : var + 1, :] = value[o : o + 1]
        return carry

    def loop(count, body, carry):
        if count == 1:
            return body(0, carry)
        return lax.fori_loop(0, count, body, carry)

    loop(groups, make_lists, 0)
    tab_in[me] = tab_out[me_owner]

    pl.semaphore_wait(barrier, devices - 1)

    other_half = pl.multiple_of((1 - comp) * half, half)
    my_half = pl.multiple_of(comp * half, half)
    partner = {"comp": 1 - comp}
    part_copies = [
        pltpu.make_async_remote_copy(
            src_ref=source.at[pl.ds(other_half, half)],
            dst_ref=target.at[comp],
            send_sem=part_sem.at[2 * k],
            recv_sem=part_sem.at[2 * k + 1],
            device_id=partner,
            device_id_type=MESH,
        )
        for k, (source, target) in enumerate(((pos, posb), (area, areab)))
    ]

    def spread_lists(source, target, send, recv, by_owner):
        def body(step, carry):
            to = (me + step) % devices
            pltpu.make_async_remote_copy(
                src_ref=source.at[to % owners if by_owner else to],
                dst_ref=target.at[me],
                send_sem=list_sem.at[send],
                recv_sem=list_sem.at[recv],
                device_id=place(to),
                device_id_type=MESH,
            ).start()
            return carry

        lax.fori_loop(1, devices, body, 0)

    def wait_lists(target, sem):
        whole = target.at[pl.ds(0, devices - 1)]
        pltpu.make_async_copy(whole, whole, list_sem.at[sem]).wait()

    spread_lists(tab_out, tab_in, 0, 1, True)
    for copy in part_copies:
        copy.start()

    sub_iota = lax.broadcasted_iota(jnp.int32, (slab, SUBS, LANES), 1)
    lane_iota = lax.broadcasted_iota(jnp.int32, (slab, SUBS, LANES), 2)
    tile_iota = lax.broadcasted_iota(jnp.int32, (slab, SUBS, LANES), 0)

    def turn(value, shift, axis):
        return value if shift == 0 else pltpu.roll(value, shift, axis)

    links = (
        (row_s, row_r, 0, tile > 0, tile < n_tile - 1, "tile", tile),
        (col_s, col_r, 2, sub > 0, sub < n_sub - 1, "sub", sub),
    )

    def halo_copy(turn_no, link, side):
        sends, receives, base, _, _, axis, place_at = link
        return pltpu.make_async_remote_copy(
            src_ref=sends.at[turn_no, side],
            dst_ref=receives.at[turn_no, 1 - side],
            send_sem=halo_send.at[turn_no, base + side],
            recv_sem=halo_recv.at[turn_no, base + 1 - side],
            device_id={axis: place_at + (1 if side else -1)},
            device_id_type=MESH,
        )

    def send_halos(turn_no, source):
        first = jnp.zeros((slab, SUBS, LANES), F32)
        last = first
        col_first = jnp.zeros((SUBS, LANES), F32)
        col_last = col_first
        for j in range(SUBS):
            block = source[j * slab : (j + 1) * slab]
            first = jnp.where(sub_iota == j, turn(block, j, 1), first)
            last = jnp.where(sub_iota == j, turn(block, (j + 1) % SUBS, 1), last)
            here = lane_iota == tile_iota + j * slab
            shape = (slab, SUBS, LANES)
            left = jnp.broadcast_to(block[:, :, 0:1], shape)
            right = jnp.broadcast_to(block[:, :, LANES - 1 : LANES], shape)
            col_first = col_first + jnp.sum(jnp.where(here, left, 0.0), axis=0)
            col_last = col_last + jnp.sum(jnp.where(here, right, 0.0), axis=0)
        row_s[turn_no, 0] = first
        row_s[turn_no, 1] = last
        col_s[turn_no, 0] = col_first
        col_s[turn_no, 1] = col_last
        for link in links:
            for side in range(2):
                receives, there = link[1], link[3 + side]

                @pl.when(there)
                def _():
                    halo_copy(turn_no, link, side).start()

                @pl.when(jnp.logical_not(there))
                def _():
                    receives[turn_no, side] = jnp.zeros(receives.shape[2:], F32)

    def wait_halos(turn_no):
        for link in links:
            for side in range(2):

                @pl.when(link[3 + side])
                def _():
                    halo_copy(turn_no, link, 1 - side).wait_recv()

    def finish_halos(turn_no):
        for link in links:
            for side in range(2):

                @pl.when(link[3 + side])
                def _():
                    halo_copy(turn_no, link, side).wait_send()

    def smooth(turn_no, source, target, subtract):
        up_rows, down_rows = row_r[turn_no, 0], row_r[turn_no, 1]
        left_cols, right_cols = (
            jnp.broadcast_to(col_r[turn_no, side][None], (slab, SUBS, LANES)).reshape(
                slab * SUBS, LANES
            )
            for side in range(2)
        )
        for j in range(SUBS):
            block = source[j * slab : (j + 1) * slab]
            at = (tile_iota + j * slab).reshape(slab * SUBS, LANES)
            left_halo = lane_gather(left_cols, at).reshape(slab, SUBS, LANES)
            right_halo = lane_gather(right_cols, at).reshape(slab, SUBS, LANES)
            up = jnp.where(sub_iota == 0, turn(up_rows, (SUBS - j) % SUBS, 1), turn(block, 1, 1))
            down = jnp.where(
                sub_iota == SUBS - 1, turn(down_rows, SUBS - 1 - j, 1), turn(block, SUBS - 1, 1)
            )
            left = jnp.where(lane_iota == 0, left_halo, turn(block, 1, 2))
            right = jnp.where(lane_iota == LANES - 1, right_halo, turn(block, LANES - 1, 2))
            result = block + SMOOTH_RATE * ((down + up + right + left) - 4.0 * block)
            if subtract is not None:
                result = result - subtract[j * slab : (j + 1) * slab]
            target[j * slab : (j + 1) * slab] = result

    send_halos(0, tr)

    posb[comp] = pos[pl.ds(my_half, half), :]
    areab[comp] = area[pl.ds(my_half, half), :]

    wait_halos(0)
    smooth(0, tr, once, None)
    send_halos(1, once)

    for copy in part_copies:
        copy.wait_recv()
    row_number = (
        (lax.broadcasted_iota(jnp.int32, (half, LANES), 0) + my_half) * LANES
        + lax.broadcasted_iota(jnp.int32, (half, LANES), 1)
    )
    live = (row_number < row_count[0]) & (sea[pl.ds(my_half, half), :] == 1)
    for c in range(2):
        wgt[c] = jnp.where(live, areab[c], 0.0)

    wait_lists(tab_in, 1)
    sub8 = lax.broadcasted_iota(jnp.int32, (SUBS, LANES), 0)
    upper = sub8 < 4
    quarter = sub8 & 3

    def join_tables(s, carry):
        tabs[s] = jnp.concatenate([tab_in[s], tab_in[owners + s]], axis=0)
        return carry

    if groups == 1:
        for s in range(owners):
            join_tables(s, 0)
    else:
        lax.fori_loop(0, owners, join_tables, 0)
    acc[...] = jnp.zeros_like(acc)

    def rows_step(step, carry):
        start = pl.multiple_of(step * SUBS, SUBS)
        at = pl.ds(start, SUBS)
        at_half = pl.ds(pl.multiple_of(my_half + step * SUBS, SUBS), SUBS)
        places = [posb[c, at, :] for c in range(2)]
        weights = [wgt[c, at, :] for c in range(2)]
        coefs = [coef[v, at_half, :] for v in range(nvar)]
        lows, highs, hots = [], [], [[], []]
        for j in range(SUBS):
            p = jnp.where(upper, row_of(places[0], j, SUBS), row_of(places[1], j, SUBS))
            lows.append(p & (LANES - 1))
            highs.append(p >> 7)
            for c in range(2):
                hots[c].append(one_hot((places[c] & (LANES - 1))[j : j + 1]))

        def find(group, found):
            found = list(found)
            for k in range(SUBS):
                s = group * SUBS + k
                table = tabs[s]
                for j in range(SUBS):
                    found[j] = jnp.where(highs[j] == s, lane_gather(table, lows[j]), found[j])
            return tuple(found)

        found = loop(groups, find, tuple(jnp.zeros((SUBS, LANES), F32) for _ in range(SUBS)))
        terms, sources = [], []
        for j in range(SUBS):
            own = found[j]
            other = pltpu.roll(own, 4, 0)
            k = row_of(coefs[nvar - 1], j, SUBS)
            for v in range(nvar - 1):
                k = jnp.where(quarter == v, row_of(coefs[v], j, SUBS), k)
            w = jnp.where(upper, row_of(weights[0], j, SUBS), row_of(weights[1], j, SUBS))
            both = row_of(own + other, nvar, SUBS)
            flux = k * (other - own) / (1.0 + k * both) * w
            main = flux.astype(BF16).astype(F32)
            terms.append(jnp.concatenate([main, flux - main], axis=0).astype(BF16))
            sources.append(
                jnp.concatenate([highs[j], highs[j]], axis=0).astype(F32).astype(BF16)
            )
        hot = [jnp.concatenate(hots[c], axis=1) for c in range(2)]

        def add(group, carry):
            none = jnp.zeros((16, LANES), BF16)
            columns = []
            for j in range(SUBS):
                columns.append(
                    jnp.concatenate(
                        [
                            jnp.where(
                                sources[j]
                                == jnp.full((16, LANES), group * SUBS + k, jnp.int32)
                                .astype(F32)
                                .astype(BF16),
                                terms[j],
                                none,
                            )
                            for k in range(SUBS)
                        ],
                        axis=0,
                    )
                )
            a = jnp.concatenate(columns, axis=1)
            for c in range(2):
                acc[c, group] += contract_lanes(a, hot[c])
            return carry

        loop(groups, add, 0)
        return carry

    lax.fori_loop(0, half // SUBS, rows_step, 0)

    def give_back(group, carry):
        for c in range(2):
            for k in range(SUBS):
                base = 16 * k + 4 * c
                total = acc[c, group, base : base + 4, :] + acc[c, group, base + 8 : base + 12, :]
                ret_out[c * owners + group * SUBS + k] = total
        return carry

    loop(groups, give_back, 0)
    ret_in[me] = ret_out[me]
    spread_lists(ret_out, ret_in, 2, 3, False)

    wait_halos(1)
    smooth(1, once, dif, tr)

    cells[...] = jnp.zeros_like(cells)
    wait_lists(ret_in, 3)

    def cells_step(group, carry):
        start = pl.multiple_of(group * SUBS, SUBS)
        cell = send_cell[pl.ds(start, SUBS), :]
        low, high = cell & (LANES - 1), cell >> 7
        columns, hot = [], []
        for j in range(SUBS):
            value = ret_in[start + j] + ret_in[owners + start + j]
            mask = row_of(high, j, SUBS) == sub8
            hot.append(one_hot(low[j : j + 1]))
            parts = []
            for _ in range(3):
                part = value.astype(BF16).astype(F32)
                value = value - part
                for v in range(4):
                    parts.append(jnp.where(mask, row_of(part, v, SUBS), 0.0))
            columns.append(jnp.concatenate(parts, axis=0).astype(BF16))
        cells[...] += contract_lanes(
            jnp.concatenate(columns, axis=1), jnp.concatenate(hot, axis=1)
        )
        return carry

    loop(groups, cells_step, 0)
    for var in range(nvar):
        parts = [cells[32 * k + 8 * var : 32 * k + 8 * var + 8, :] for k in range(3)]
        flux = parts[0] + (parts[1] + parts[2])
        last = var * nlev + nlev - 1
        column = surface[var] + surface[nvar] * flux
        out[last] = column + dif[last]
        for level in range(nlev - 2, -1, -1):
            n = var * nlev + level
            column = off[n] + fac[level] * column
            out[n] = column + dif[n]

    for copy in part_copies:
        copy.wait_send()
    finish_halos(0)
    finish_halos(1)
    wait_lists(tab_in, 0)
    wait_lists(ret_in, 2)


def per_device(
    n_tile, n_sub, tracers, couple, send_cell, recv_pos, row_count, sea_mask, exch_coef, margin_area
):
    nvar, nlev = tracers.shape[1:3]
    tiles = nvar * nlev
    owners = n_tile * n_sub
    rows = recv_pos.shape[-1] // LANES
    slab = tiles // SUBS
    block = (SUBS, LANES)
    vmem = pl.BlockSpec(memory_space=pltpu.VMEM)
    scratch = [
        pltpu.VMEM((tiles,) + block, F32),
        pltpu.VMEM((nlev,) + block, F32),
        pltpu.VMEM((tiles,) + block, F32),
        pltpu.VMEM((tiles,) + block, F32),
        pltpu.VMEM((owners, 4, LANES), F32),
        pltpu.VMEM((2 * owners, 4, LANES), F32),
        pltpu.VMEM((owners,) + block, F32),
        pltpu.VMEM((2, rows // 2, LANES), jnp.int32),
        pltpu.VMEM((2, rows // 2, LANES), F32),
        pltpu.VMEM((2, rows // 2, LANES), F32),
        pltpu.VMEM((2, owners // SUBS, 16 * SUBS, LANES), F32),
        pltpu.VMEM((2 * owners, 4, LANES), F32),
        pltpu.VMEM((2 * owners, 4, LANES), F32),
        pltpu.VMEM((2, 2, slab) + block, F32),
        pltpu.VMEM((2, 2, slab) + block, F32),
        pltpu.VMEM((2, 2) + block, F32),
        pltpu.VMEM((2, 2) + block, F32),
        pltpu.VMEM((96, LANES), F32),
        pltpu.SemaphoreType.DMA((4,)),
        pltpu.SemaphoreType.DMA((2, 4)),
        pltpu.SemaphoreType.DMA((2, 4)),
        pltpu.SemaphoreType.DMA((4,)),
    ]
    updated = pl.pallas_call(
        functools.partial(kernel, n_tile, n_sub, nvar, nlev),
        out_shape=jax.ShapeDtypeStruct((tiles,) + block, F32),
        in_specs=[vmem] * 4 + [pl.BlockSpec(memory_space=pltpu.SMEM)] + [vmem] * 3,
        out_specs=vmem,
        scratch_shapes=scratch,
        compiler_params=pltpu.CompilerParams(
            collective_id=0, has_side_effects=True, vmem_limit_bytes=32 * 1024 * 1024
        ),
        name="coupled_step",
    )(
        tracers.reshape((tiles,) + block),
        couple.reshape((nlev,) + block),
        send_cell.reshape(owners, LANES),
        recv_pos.reshape(rows, LANES),
        row_count,
        sea_mask.reshape(rows, LANES),
        exch_coef.reshape(nvar, rows, LANES),
        margin_area.reshape(rows, LANES),
    )
    return updated.reshape(tracers.shape)


def solution(mesh):
    placed = (
        P("comp", "member", None, "tile", "sub"),
        P("comp", "member", "tile", "sub"),
        P("comp", ("tile", "sub"), None, None),
        P("comp", ("tile", "sub"), None),
        P(("tile", "sub")),
        P(("tile", "sub"), None),
        P("member", ("tile", "sub"), None),
        P("comp", ("tile", "sub"), None),
    )
    return jax.shard_map(
        functools.partial(per_device, mesh.shape["tile"], mesh.shape["sub"]),
        mesh=mesh,
        in_specs=placed,
        out_specs=P("comp", "member", None, "tile", "sub"),
        check_vma=False,
    )
```

time: 241 us -> 26.8 us (0.11)
  other arithmetic: 112 us -> 0 us
  local copies, waits for them, and re-layouts: 83.4 us -> 6.77 us
  starting transfers between devices: 36.6 us -> 0 us
  Pallas kernels: 0 us -> 19 us
  waiting for transfers between devices: 6.48 us -> 0 us
    scatter-add x2 -> x0, other arithmetic: 94 us -> none  [the longest x1 87.7 us: per_device(): jax.ops.segment_sum(flux.T, positions, num_segments=owners * slot_count)]
    gather x4 -> x0, local copies, waits for them, and re-layouts: 63.9 us -> none  [the longest x2 60.2 us: per_device(): own_rows = jnp.take(received, positions, axis=0).T]
    ppermute x9 -> x0, starting transfers between devices: 23.4 us -> none  [the longest x4 18.2 us: extended(): before = lax.ppermute(last, axis, up)]
    pallas_call x0 -> x1, Pallas kernels: none -> 19 us  [per_device(): pl.pallas_call(functools.partial(kernel, n_tile, n_sub, nvar, nlev), out_...]
    all_to_all x2 -> x0, starting transfers between devices: 13.2 us -> none  [the longest x1 7.27 us: per_device(): lax.all_to_all(outgoing, ('tile', 'sub'), split_axis=0, concat_axis=0, ti...]
    squeeze x4 -> x0, local copies, waits for them, and re-layouts: 5.88 us -> none  [per_device(): couple_below = coupling[level + 1] if level + 1 < nlev else zeros_plane]
    div x19 -> x0, other arithmetic: 5.73 us -> none  [the longest x16 4.43 us: per_device(): factors.append(couple_below / pivot)]
    transpose x1 -> x0, local copies, waits for them, and re-layouts: 5.09 us -> none  [per_device(): slot_sums = jax.ops.segment_sum(flux.T, positions, num_segments=owners *...]
  transfers between devices with their start and end apart: 11 -> 0, of which waited for: 2 -> 0; matrix products, arithmetic and copies ran while one was open for 68% -> 0% of each run, Pallas kernels for 0% -> 0%
where the time goes in v1:
time: 26.8 us; the launch traced here: 26.4 us
  Pallas kernels  19 us (71%)
  local copies, waits for them, and re-layouts  6.77 us (25%)
  between operations  0.67 us (2%)
    pallas_call x1, Pallas kernels, per_device(): pl.pallas_call(functools.partial(kernel, n_tile, n_sub, nvar, nlev), out_...  19 us
    unnamed x15, local copies, waits for them, and re-layouts  6.77 us

profile of v1, /device:TPU:0, one launch (start us, length us, event | category | flops | bytes accessed | tf_op | source)
XLA Modules:
  0.0 26.4 jit_solution(9127526450759918845)
XLA Ops:
  0.7 0.0 copy-start.6
  0.7 0.7 %copy-done.6 = s32[1,1,8,128]{3,2,1,0:T(8,128)S(1)} copy-done((s32[1,1,8,128]{3,2,1,0:T(8,128)S(1)}, s32[1,1,8,128]{3,2,1,0:T(8,128)}, u32[]{:S(2)}) %copy-start.6) | copy-done | bytes 4120
  1.3 0.0 copy-start
  1.3 1.0 %copy-done = f32[1,3,32,8,128]{4,3,2,1,0:T(8,128)S(1)} copy-done((f32[1,3,32,8,128]{4,3,2,1,0:T(8,128)S(1)}, f32[1,3,32,8,128]{4,3,2,1,0:T(8,128)}, u32[]{:S(2)}) %copy-start) | copy-done | bytes 393240
  2.3 0.0 copy-start.1
  2.3 0.9 %copy-done.1 = f32[3,1,16384]{2,1,0:T(1,128)S(1)} copy-done((f32[3,1,16384]{2,1,0:T(1,128)S(1)}, f32[3,1,16384]{2,1,0:T(1,128)}, u32[]{:S(2)}) %copy-start.1) | copy-done | bytes 196632
  3.3 0.0 copy-start.2
  3.3 0.9 %copy-done.2 = f32[1,32,8,128]{3,2,1,0:T(8,128)S(1)} copy-done((f32[1,32,8,128]{3,2,1,0:T(8,128)S(1)}, f32[1,32,8,128]{3,2,1,0:T(8,128)}, u32[]{:S(2)}) %copy-start.2) | copy-done | bytes 131096
  4.2 0.0 copy-start.3
  4.2 0.8 %copy-done.3 = s32[1,1,16384]{2,1,0:T(1,128)S(1)} copy-done((s32[1,1,16384]{2,1,0:T(1,128)S(1)}, s32[1,1,16384]{2,1,0:T(1,128)}, u32[]{:S(2)}) %copy-start.3) | copy-done | bytes 65560
  5.0 0.0 copy-start.4
  5.0 0.8 %copy-done.4 = s32[1,16384]{1,0:T(1,128)S(1)} copy-done((s32[1,16384]{1,0:T(1,128)S(1)}, s32[1,16384]{1,0:T(1,128)}, u32[]{:S(2)}) %copy-start.4) | copy-done | bytes 65560
  5.8 0.0 copy-start.5
  5.9 0.8 %copy-done.5 = f32[1,1,16384]{2,1,0:T(1,128)S(1)} copy-done((f32[1,1,16384]{2,1,0:T(1,128)S(1)}, f32[1,1,16384]{2,1,0:T(1,128)}, u32[]{:S(2)}) %copy-start.5) | copy-done | bytes 65560
  6.7 19.0 %coupled_step.1 = f32[96,8,128]{2,1,0:T(8,128)S(1)} custom-call(f32[96,8,128]{2,1,0:T(8,128)S(1)} %bitcast.9, f32[32,8,128]{2,1,0:T(8,128)S(1)} %bitcast.11, s32[8,128]{1,0:T(8,128)S(1)} %bitcast.15, s32[128,128]{1,0:T(8,128)S(1)} %bitcast.12, s32[1]{0:T(128)S(6)} %copy.10.row_count, s32[128,128]{1,0:T(8,128)S(1)} %bitcast.13, f32[3,128,128]{2,1,0:T(8,128)S(1)} %bitcast.10, ...), custom_call_target="tpu_custom_call" | custom-call | tf_op jit(solution)/shard_map/coupled_step/pallas_call | solution.py:448
  25.7 0.7 %copy.11 = f32[1,3,32,8,128]{4,3,2,1,0:T(8,128)} copy(f32[1,3,32,8,128]{4,3,2,1,0:T(8,128)S(1)} %bitcast.8) | data formatting | bytes 786432
Async XLA Ops:
  0.7 0.7 %copy-start.6 = (s32[1,1,8,128]{3,2,1,0:T(8,128)S(1)}, s32[1,1,8,128]{3,2,1,0:T(8,128)}, u32[]{:S(2)}) copy-start(s32[1,1,8,128]{3,2,1,0:T(8,128)} %param.10) | copy-start | bytes 12292
  1.3 1.0 %copy-start = (f32[1,3,32,8,128]{4,3,2,1,0:T(8,128)S(1)}, f32[1,3,32,8,128]{4,3,2,1,0:T(8,128)}, u32[]{:S(2)}) copy-start(f32[1,3,32,8,128]{4,3,2,1,0:T(8,128)} %param.8) | copy-start | bytes 1179652
  2.3 0.9 %copy-start.1 = (f32[3,1,16384]{2,1,0:T(1,128)S(1)}, f32[3,1,16384]{2,1,0:T(1,128)}, u32[]{:S(2)}) copy-start(f32[3,1,16384]{2,1,0:T(1,128)} %param.14) | copy-start | bytes 589828
  3.3 0.9 %copy-start.2 = (f32[1,32,8,128]{3,2,1,0:T(8,128)S(1)}, f32[1,32,8,128]{3,2,1,0:T(8,128)}, u32[]{:S(2)}) copy-start(f32[1,32,8,128]{3,2,1,0:T(8,128)} %param.9) | copy-start | bytes 393220
  4.2 0.8 %copy-start.3 = (s32[1,1,16384]{2,1,0:T(1,128)S(1)}, s32[1,1,16384]{2,1,0:T(1,128)}, u32[]{:S(2)}) copy-start(s32[1,1,16384]{2,1,0:T(1,128)} %param.11) | copy-start | bytes 196612
  5.0 0.8 %copy-start.4 = (s32[1,16384]{1,0:T(1,128)S(1)}, s32[1,16384]{1,0:T(1,128)}, u32[]{:S(2)}) copy-start(s32[1,16384]{1,0:T(1,128)} %param.13) | copy-start | bytes 196612
  5.8 0.8 %copy-start.5 = (f32[1,1,16384]{2,1,0:T(1,128)S(1)}, f32[1,1,16384]{2,1,0:T(1,128)}, u32[]{:S(2)}) copy-start(f32[1,1,16384]{2,1,0:T(1,128)} %param.15) | copy-start | bytes 196612

commit v2 on v1

--- a/solution.py
+++ b/solution.py
@@ -41,8 +41,9 @@
 
 def kernel(
     n_tile, n_sub, nvar, nlev,
-    tr, couple, send_cell, pos, row_count, sea, coef, area,
+    tr_hbm, couple_hbm, cell_hbm, pos, row_count, sea_hbm, coef_hbm, area,
     out,
+    tr, couple, send_cell, sea, coef, load_sem,
     off, fac, once, dif, tab_out, tab_in, tabs, posb, areab, wgt, acc, ret_out, ret_in,
     row_s, row_r, col_s, col_r, cells,
     part_sem, halo_send, halo_recv, list_sem,
@@ -57,6 +58,26 @@
     me_owner = tile * n_sub + sub
     me = comp * owners + me_owner
 
+    other_half = pl.multiple_of((1 - comp) * half, half)
+    my_half = pl.multiple_of(comp * half, half)
+    mine = pl.ds(my_half, half)
+    loads = [
+        pltpu.make_async_copy(source, target, load_sem.at[k])
+        for k, (source, target) in enumerate(
+            (
+                (couple_hbm, couple),
+                (tr_hbm, tr),
+                (cell_hbm, send_cell),
+                (pos.at[mine], posb.at[comp]),
+                (area.at[mine], areab.at[comp]),
+                (sea_hbm.at[mine], sea),
+                (coef_hbm.at[:, mine], coef),
+            )
+        )
+    ]
+    for copy in loads:
+        copy.start()
+
     def place(index):
         owner = index % owners
         return {"comp": index // owners, "tile": owner // n_sub, "sub": owner % n_sub}
@@ -71,6 +92,8 @@
 
     lax.fori_loop(1, devices, greet, 0)
 
+    loads[0].wait()
+    loads[1].wait()
     factor = None
     offset = [None] * nvar
     for level in range(nlev):
@@ -90,6 +113,8 @@
         fac[level] = factor
     surface = offset + [inverse]
 
+    loads[2].wait()
+
     def make_lists(group, carry):
         start = pl.multiple_of(group * SUBS, SUBS)
         cell = send_cell[pl.ds(start, SUBS), :]
@@ -113,8 +138,6 @@
 
     pl.semaphore_wait(barrier, devices - 1)
 
-    other_half = pl.multiple_of((1 - comp) * half, half)
-    my_half = pl.multiple_of(comp * half, half)
     partner = {"comp": 1 - comp}
     part_copies = [
         pltpu.make_async_remote_copy(
@@ -247,20 +270,19 @@
 
     send_halos(0, tr)
 
-    posb[comp] = pos[pl.ds(my_half, half), :]
-    areab[comp] = area[pl.ds(my_half, half), :]
-
     wait_halos(0)
     smooth(0, tr, once, None)
     send_halos(1, once)
 
+    for copy in loads[3:]:
+        copy.wait()
     for copy in part_copies:
         copy.wait_recv()
     row_number = (
         (lax.broadcasted_iota(jnp.int32, (half, LANES), 0) + my_half) * LANES
         + lax.broadcasted_iota(jnp.int32, (half, LANES), 1)
     )
-    live = (row_number < row_count[0]) & (sea[pl.ds(my_half, half), :] == 1)
+    live = (row_number < row_count[0]) & (sea[...] == 1)
     for c in range(2):
         wgt[c] = jnp.where(live, areab[c], 0.0)
 
@@ -283,10 +305,9 @@
     def rows_step(step, carry):
         start = pl.multiple_of(step * SUBS, SUBS)
         at = pl.ds(start, SUBS)
-        at_half = pl.ds(pl.multiple_of(my_half + step * SUBS, SUBS), SUBS)
         places = [posb[c, at, :] for c in range(2)]
         weights = [wgt[c, at, :] for c in range(2)]
-        coefs = [coef[v, at_half, :] for v in range(nvar)]
+        coefs = [coef[v, at, :] for v in range(nvar)]
         lows, highs, hots = [], [], [[], []]
         for j in range(SUBS):
             p = jnp.where(upper, row_of(places[0], j, SUBS), row_of(places[1], j, SUBS))
@@ -421,7 +442,14 @@
     slab = tiles // SUBS
     block = (SUBS, LANES)
     vmem = pl.BlockSpec(memory_space=pltpu.VMEM)
+    hbm = pl.BlockSpec(memory_space=pltpu.HBM)
     scratch = [
+        pltpu.VMEM((tiles,) + block, F32),
+        pltpu.VMEM((nlev,) + block, F32),
+        pltpu.VMEM((owners, LANES), jnp.int32),
+        pltpu.VMEM((rows // 2, LANES), jnp.int32),
+        pltpu.VMEM((nvar, rows // 2, LANES), F32),
+        pltpu.SemaphoreType.DMA((7,)),
         pltpu.VMEM((tiles,) + block, F32),
         pltpu.VMEM((nlev,) + block, F32),
         pltpu.VMEM((tiles,) + block, F32),
@@ -448,11 +476,11 @@
     updated = pl.pallas_call(
         functools.partial(kernel, n_tile, n_sub, nvar, nlev),
         out_shape=jax.ShapeDtypeStruct((tiles,) + block, F32),
-        in_specs=[vmem] * 4 + [pl.BlockSpec(memory_space=pltpu.SMEM)] + [vmem] * 3,
+        in_specs=[hbm] * 4 + [pl.BlockSpec(memory_space=pltpu.SMEM)] + [hbm] * 3,
         out_specs=vmem,
         scratch_shapes=scratch,
         compiler_params=pltpu.CompilerParams(
-            collective_id=0, has_side_effects=True, vmem_limit_bytes=32 * 1024 * 1024
+            collective_id=0, has_side_effects=True, vmem_limit_bytes=63 * 1024 * 1024
         ),
         name="coupled_step",
     )(

time: 26.8 us -> 22.6 us (0.84)
  local copies, waits for them, and re-layouts: 6.77 us -> 1.77 us
  Pallas kernels: 19 us -> 20 us
    unnamed x15 -> x1, local copies, waits for them, and re-layouts: 6.77 us -> 1.77 us
    pallas_call x1, Pallas kernels: 19 us -> 20 us  [per_device(): pl.pallas_call(functools.partial(kernel, n_tile, n_sub, nvar, nlev), out_...]
where the time goes in v2:
time: 22.6 us; the launch traced here: 22.4 us
  Pallas kernels  20 us (88%)
  local copies, waits for them, and re-layouts  1.77 us (8%)
  between operations  0.66 us (3%)
    pallas_call x1, Pallas kernels, per_device(): pl.pallas_call(functools.partial(kernel, n_tile, n_sub, nvar, nlev), out_...  20 us
    unnamed x1, local copies, waits for them, and re-layouts  1.77 us

profile of v2, /device:TPU:0, one launch (start us, length us, event | category | flops | bytes accessed | tf_op | source)
XLA Modules:
  0.0 22.4 jit_solution(7992585533562739709)
XLA Ops:
  0.7 20.0 %coupled_step.1 = f32[96,8,128]{2,1,0:T(8,128)} custom-call(f32[96,8,128]{2,1,0:T(8,128)} %bitcast.9, f32[32,8,128]{2,1,0:T(8,128)} %bitcast.11, s32[8,128]{1,0:T(8,128)} %bitcast.15, s32[128,128]{1,0:T(8,128)} %bitcast.12, s32[1]{0:T(128)S(6)} %copy.10.row_count, s32[128,128]{1,0:T(8,128)} %bitcast.13, f32[3,128,128]{2,1,0:T(8,128)} %bitcast.10, ...), custom_call_target="tpu_custom_call" | custom-call | tf_op jit(solution)/shard_map/coupled_step/pallas_call | solution.py:476
  20.6 1.8 %copy.11 = f32[1,3,32,8,128]{4,3,2,1,0:T(8,128)} copy(f32[1,3,32,8,128]{4,3,2,1,0:T(8,128)} %bitcast.8) | data formatting | bytes 786432

commit v3 on v2

--- a/solution.py
+++ b/solution.py
@@ -44,7 +44,7 @@
     tr_hbm, couple_hbm, cell_hbm, pos, row_count, sea_hbm, coef_hbm, area,
     out,
     tr, couple, send_cell, sea, coef, load_sem,
-    off, fac, once, dif, tab_out, tab_in, tabs, posb, areab, wgt, acc, ret_out, ret_in,
+    off, fac, once, dif, gain, hots, cell_hots, tab_out, tab_in, tabs, posb, areab, wgt, acc, ret_out, ret_in,
     row_s, row_r, col_s, col_r, cells,
     part_sem, halo_send, halo_recv, list_sem,
 ):
@@ -84,13 +84,34 @@
 
     barrier = pltpu.get_barrier_semaphore()
 
-    def greet(step, carry):
-        pl.semaphore_signal(
-            barrier, inc=1, device_id=place((me + step) % devices), device_id_type=MESH
-        )
-        return carry
-
-    lax.fori_loop(1, devices, greet, 0)
+    def step_on(value, step, size):
+        moved = value + step
+        return jnp.where(moved >= size, moved - size, moved) if step else value
+
+    def each_other(visit):
+        if devices <= 32:
+            for b in range(n_tile):
+                for d in range(n_sub):
+                    for a in range(2):
+                        if a or b or d:
+                            to_comp = step_on(comp, a, 2)
+                            to_tile, to_sub = step_on(tile, b, n_tile), step_on(sub, d, n_sub)
+                            at = {"comp": to_comp, "tile": to_tile, "sub": to_sub}
+                            owner = to_tile * n_sub + to_sub
+                            visit(at, owner, to_comp * owners + owner)
+        else:
+
+            def body(step, carry):
+                to = (me + step) % devices
+                visit(place(to), to % owners, to)
+                return carry
+
+            lax.fori_loop(1, devices, body, 0)
+
+    def greet(at, owner, index):
+        pl.semaphore_signal(barrier, inc=1, device_id=at, device_id_type=MESH)
+
+    each_other(greet)
 
     loads[0].wait()
     loads[1].wait()
@@ -152,19 +173,17 @@
     ]
 
     def spread_lists(source, target, send, recv, by_owner):
-        def body(step, carry):
-            to = (me + step) % devices
+        def visit(at, owner, index):
             pltpu.make_async_remote_copy(
-                src_ref=source.at[to % owners if by_owner else to],
+                src_ref=source.at[owner if by_owner else index],
                 dst_ref=target.at[me],
                 send_sem=list_sem.at[send],
                 recv_sem=list_sem.at[recv],
-                device_id=place(to),
+                device_id=at,
                 device_id_type=MESH,
             ).start()
-            return carry
-
-        lax.fori_loop(1, devices, body, 0)
+
+        each_other(visit)
 
     def wait_lists(target, sem):
         whole = target.at[pl.ds(0, devices - 1)]
@@ -270,14 +289,34 @@
 
     send_halos(0, tr)
 
-    wait_halos(0)
-    smooth(0, tr, once, None)
-    send_halos(1, once)
-
     for copy in loads[3:]:
         copy.wait()
     for copy in part_copies:
         copy.wait_recv()
+
+    def make_hots(step, carry):
+        at = pl.ds(pl.multiple_of(step * SUBS, SUBS), SUBS)
+        for c in range(2):
+            low = posb[c, at, :] & (LANES - 1)
+            for j in range(SUBS):
+                hots[c, step, :, j * LANES : (j + 1) * LANES] = one_hot(low[j : j + 1])
+        return carry
+
+    lax.fori_loop(0, half // SUBS, make_hots, 0)
+
+    def make_cell_hots(group, carry):
+        start = pl.multiple_of(group * SUBS, SUBS)
+        low = send_cell[pl.ds(start, SUBS), :] & (LANES - 1)
+        for j in range(SUBS):
+            cell_hots[group, :, j * LANES : (j + 1) * LANES] = one_hot(low[j : j + 1])
+        return carry
+
+    loop(groups, make_cell_hots, 0)
+
+    wait_halos(0)
+    smooth(0, tr, once, None)
+    send_halos(1, once)
+
     row_number = (
         (lax.broadcasted_iota(jnp.int32, (half, LANES), 0) + my_half) * LANES
         + lax.broadcasted_iota(jnp.int32, (half, LANES), 1)
@@ -308,13 +347,11 @@
         places = [posb[c, at, :] for c in range(2)]
         weights = [wgt[c, at, :] for c in range(2)]
         coefs = [coef[v, at, :] for v in range(nvar)]
-        lows, highs, hots = [], [], [[], []]
+        lows, highs = [], []
         for j in range(SUBS):
             p = jnp.where(upper, row_of(places[0], j, SUBS), row_of(places[1], j, SUBS))
             lows.append(p & (LANES - 1))
             highs.append(p >> 7)
-            for c in range(2):
-                hots[c].append(one_hot((places[c] & (LANES - 1))[j : j + 1]))
 
         def find(group, found):
             found = list(found)
@@ -341,7 +378,6 @@
             sources.append(
                 jnp.concatenate([highs[j], highs[j]], axis=0).astype(F32).astype(BF16)
             )
-        hot = [jnp.concatenate(hots[c], axis=1) for c in range(2)]
 
         def add(group, carry):
             none = jnp.zeros((16, LANES), BF16)
@@ -365,7 +401,7 @@
                 )
             a = jnp.concatenate(columns, axis=1)
             for c in range(2):
-                acc[c, group] += contract_lanes(a, hot[c])
+                acc[c, group] += contract_lanes(a, hots[c, step])
             return carry
 
         loop(groups, add, 0)
@@ -388,18 +424,31 @@
     wait_halos(1)
     smooth(1, once, dif, tr)
 
+    slope = surface[nvar]
+    gain[nlev - 1] = slope
+    for level in range(nlev - 2, -1, -1):
+        slope = fac[level] * slope
+        gain[level] = slope
+    for var in range(nvar):
+        last = var * nlev + nlev - 1
+        column = surface[var]
+        off[last] = column + dif[last]
+        for level in range(nlev - 2, -1, -1):
+            n = var * nlev + level
+            column = off[n] + fac[level] * column
+            off[n] = column + dif[n]
+
     cells[...] = jnp.zeros_like(cells)
     wait_lists(ret_in, 3)
 
     def cells_step(group, carry):
         start = pl.multiple_of(group * SUBS, SUBS)
         cell = send_cell[pl.ds(start, SUBS), :]
-        low, high = cell & (LANES - 1), cell >> 7
-        columns, hot = [], []
+        high = cell >> 7
+        columns = []
         for j in range(SUBS):
             value = ret_in[start + j] + ret_in[owners + start + j]
             mask = row_of(high, j, SUBS) == sub8
-            hot.append(one_hot(low[j : j + 1]))
             parts = []
             for _ in range(3):
                 part = value.astype(BF16).astype(F32)
@@ -408,7 +457,7 @@
                     parts.append(jnp.where(mask, row_of(part, v, SUBS), 0.0))
             columns.append(jnp.concatenate(parts, axis=0).astype(BF16))
         cells[...] += contract_lanes(
-            jnp.concatenate(columns, axis=1), jnp.concatenate(hot, axis=1)
+            jnp.concatenate(columns, axis=1), cell_hots[group]
         )
         return carry
 
@@ -416,13 +465,9 @@
     for var in range(nvar):
         parts = [cells[32 * k + 8 * var : 32 * k + 8 * var + 8, :] for k in range(3)]
         flux = parts[0] + (parts[1] + parts[2])
-        last = var * nlev + nlev - 1
-        column = surface[var] + surface[nvar] * flux
-        out[last] = column + dif[last]
-        for level in range(nlev - 2, -1, -1):
+        for level in range(nlev):
             n = var * nlev + level
-            column = off[n] + fac[level] * column
-            out[n] = column + dif[n]
+            out[n] = off[n] + gain[level] * flux
 
     for copy in part_copies:
         copy.wait_send()
@@ -454,6 +499,9 @@
         pltpu.VMEM((nlev,) + block, F32),
         pltpu.VMEM((tiles,) + block, F32),
         pltpu.VMEM((tiles,) + block, F32),
+        pltpu.VMEM((nlev,) + block, F32),
+        pltpu.VMEM((2, rows // 2 // SUBS, LANES, SUBS * LANES), BF16),
+        pltpu.VMEM((owners // SUBS, LANES, SUBS * LANES), BF16),
         pltpu.VMEM((owners, 4, LANES), F32),
         pltpu.VMEM((2 * owners, 4, LANES), F32),
         pltpu.VMEM((owners,) + block, F32),
@@ -480,18 +528,18 @@
         out_specs=vmem,
         scratch_shapes=scratch,
         compiler_params=pltpu.CompilerParams(
-            collective_id=0, has_side_effects=True, vmem_limit_bytes=63 * 1024 * 1024
+            collective_id=0, has_side_effects=True, vmem_limit_bytes=40 * 1024 * 1024
         ),
         name="coupled_step",
     )(
-        tracers.reshape((tiles,) + block),
-        couple.reshape((nlev,) + block),
-        send_cell.reshape(owners, LANES),
-        recv_pos.reshape(rows, LANES),
+        pltpu.with_memory_space_constraint(tracers.reshape((tiles,) + block), pltpu.HBM),
+        pltpu.with_memory_space_constraint(couple.reshape((nlev,) + block), pltpu.HBM),
+        pltpu.with_memory_space_constraint(send_cell.reshape(owners, LANES), pltpu.HBM),
+        pltpu.with_memory_space_constraint(recv_pos.reshape(rows, LANES), pltpu.HBM),
         row_count,
-        sea_mask.reshape(rows, LANES),
-        exch_coef.reshape(nvar, rows, LANES),
-        margin_area.reshape(rows, LANES),
+        pltpu.with_memory_space_constraint(sea_mask.reshape(rows, LANES), pltpu.HBM),
+        pltpu.with_memory_space_constraint(exch_coef.reshape(nvar, rows, LANES), pltpu.HBM),
+        pltpu.with_memory_space_constraint(margin_area.reshape(rows, LANES), pltpu.HBM),
     )
     return updated.reshape(tracers.shape)
 

time: 22.6 us -> 20.6 us (0.912)
  local copies, waits for them, and re-layouts: 1.77 us -> 0.75 us
  Pallas kernels: 20 us -> 19.1 us
    unnamed x1, local copies, waits for them, and re-layouts: 1.77 us -> 0.75 us
    pallas_call x1, Pallas kernels: 20 us -> 19.1 us  [per_device(): pl.pallas_call(functools.partial(kernel, n_tile, n_sub, nvar, nlev), out_...]
where the time goes in v3:
time: 20.6 us; the launch traced here: 20.5 us
  Pallas kernels  19.1 us (93%)
  local copies, waits for them, and re-layouts  0.75 us (4%)
  between operations  0.66 us (3%)
    pallas_call x1, Pallas kernels, per_device(): pl.pallas_call(functools.partial(kernel, n_tile, n_sub, nvar, nlev), out_...  19.1 us
    unnamed x1, local copies, waits for them, and re-layouts  0.75 us

profile of v3, /device:TPU:0, one launch (start us, length us, event | category | flops | bytes accessed | tf_op | source)
XLA Modules:
  0.0 20.5 jit_solution(4406348914326740348)
XLA Ops:
  0.7 19.1 %coupled_step.1 = f32[96,8,128]{2,1,0:T(8,128)S(1)} custom-call(f32[96,8,128]{2,1,0:T(8,128)} %bitcast.9, f32[32,8,128]{2,1,0:T(8,128)} %bitcast.11, s32[8,128]{1,0:T(8,128)} %bitcast.15, s32[128,128]{1,0:T(8,128)} %bitcast.12, s32[1]{0:T(128)S(6)} %copy.10.row_count, s32[128,128]{1,0:T(8,128)} %bitcast.13, f32[3,128,128]{2,1,0:T(8,128)} %bitcast.10, ...), custom_call_target="tpu_custom_call" | custom-call | tf_op jit(solution)/shard_map/coupled_step/pallas_call | solution.py:524
  19.7 0.7 %copy.11 = f32[1,3,32,8,128]{4,3,2,1,0:T(8,128)} copy(f32[1,3,32,8,128]{4,3,2,1,0:T(8,128)S(1)} %bitcast.8) | data formatting | bytes 786432

commit v4 on v3

--- a/solution.py
+++ b/solution.py
@@ -75,27 +75,19 @@
             )
         )
     ]
-    for copy in loads:
-        copy.start()
-
     def place(index):
         owner = index % owners
         return {"comp": index // owners, "tile": owner // n_sub, "sub": owner % n_sub}
 
     barrier = pltpu.get_barrier_semaphore()
 
-    def step_on(value, step, size):
-        moved = value + step
-        return jnp.where(moved >= size, moved - size, moved) if step else value
-
     def each_other(visit):
-        if devices <= 32:
-            for b in range(n_tile):
-                for d in range(n_sub):
+        if devices <= 32 and n_tile & (n_tile - 1) == 0 and n_sub & (n_sub - 1) == 0:
+            for b in range(n_tile - 1, -1, -1):
+                for d in range(n_sub - 1, -1, -1):
                     for a in range(2):
                         if a or b or d:
-                            to_comp = step_on(comp, a, 2)
-                            to_tile, to_sub = step_on(tile, b, n_tile), step_on(sub, d, n_sub)
+                            to_comp, to_tile, to_sub = comp ^ a, tile ^ b, sub ^ d
                             at = {"comp": to_comp, "tile": to_tile, "sub": to_sub}
                             owner = to_tile * n_sub + to_sub
                             visit(at, owner, to_comp * owners + owner)
@@ -112,6 +104,8 @@
         pl.semaphore_signal(barrier, inc=1, device_id=at, device_id_type=MESH)
 
     each_other(greet)
+    for copy in loads:
+        copy.start()
 
     loads[0].wait()
     loads[1].wait()
@@ -407,7 +401,7 @@
         loop(groups, add, 0)
         return carry
 
-    lax.fori_loop(0, half // SUBS, rows_step, 0)
+    lax.fori_loop(0, half // SUBS, rows_step, 0, unroll=4)
 
     def give_back(group, carry):
         for c in range(2):

time: 20.6 us -> 17.7 us (0.86)
  Pallas kernels: 19.1 us -> 16.1 us
    pallas_call x1, Pallas kernels: 19.1 us -> 16.1 us  [per_device(): pl.pallas_call(functools.partial(kernel, n_tile, n_sub, nvar, nlev), out_...]
where the time goes in v4:
time: 17.7 us; the launch traced here: 17.5 us
  Pallas kernels  16.1 us (91%)
  local copies, waits for them, and re-layouts  0.75 us (4%)
  between operations  0.66 us (4%)
    pallas_call x1, Pallas kernels, per_device(): pl.pallas_call(functools.partial(kernel, n_tile, n_sub, nvar, nlev), out_...  16.1 us
    unnamed x1, local copies, waits for them, and re-layouts  0.75 us

profile of v4, /device:TPU:0, one launch (start us, length us, event | category | flops | bytes accessed | tf_op | source)
XLA Modules:
  0.0 17.5 jit_solution(10287906149316803343)
XLA Ops:
  0.7 16.1 %coupled_step.1 = f32[96,8,128]{2,1,0:T(8,128)S(1)} custom-call(f32[96,8,128]{2,1,0:T(8,128)} %bitcast.9, f32[32,8,128]{2,1,0:T(8,128)} %bitcast.11, s32[8,128]{1,0:T(8,128)} %bitcast.15, s32[128,128]{1,0:T(8,128)} %bitcast.12, s32[1]{0:T(128)S(6)} %copy.10.row_count, s32[128,128]{1,0:T(8,128)} %bitcast.13, f32[3,128,128]{2,1,0:T(8,128)} %bitcast.10, ...), custom_call_target="tpu_custom_call" | custom-call | tf_op jit(solution)/shard_map/coupled_step/pallas_call | solution.py:518
  16.8 0.7 %copy.11 = f32[1,3,32,8,128]{4,3,2,1,0:T(8,128)} copy(f32[1,3,32,8,128]{4,3,2,1,0:T(8,128)S(1)} %bitcast.8) | data formatting | bytes 786432

commit v5 on v4

--- a/solution.py
+++ b/solution.py
@@ -401,7 +401,7 @@
         loop(groups, add, 0)
         return carry
 
-    lax.fori_loop(0, half // SUBS, rows_step, 0, unroll=4)
+    lax.fori_loop(0, half // SUBS, rows_step, 0, unroll=8)
 
     def give_back(group, carry):
         for c in range(2):

time: 17.7 us -> 17.4 us (0.983)
  Pallas kernels: 16.1 us -> 15.8 us
    pallas_call x1, Pallas kernels: 16.1 us -> 15.8 us  [per_device(): pl.pallas_call(functools.partial(kernel, n_tile, n_sub, nvar, nlev), out_...]
where the time goes in v5:
time: 17.4 us; the launch traced here: 17.2 us
  Pallas kernels  15.8 us (91%)
  local copies, waits for them, and re-layouts  0.75 us (4%)
  between operations  0.66 us (4%)
    pallas_call x1, Pallas kernels, per_device(): pl.pallas_call(functools.partial(kernel, n_tile, n_sub, nvar, nlev), out_...  15.8 us
    unnamed x1, local copies, waits for them, and re-layouts  0.75 us

profile of v5, /device:TPU:0, one launch (start us, length us, event | category | flops | bytes accessed | tf_op | source)
XLA Modules:
  0.0 17.2 jit_solution(17999459254302979118)
XLA Ops:
  0.7 15.8 %coupled_step.1 = f32[96,8,128]{2,1,0:T(8,128)S(1)} custom-call(f32[96,8,128]{2,1,0:T(8,128)} %bitcast.9, f32[32,8,128]{2,1,0:T(8,128)} %bitcast.11, s32[8,128]{1,0:T(8,128)} %bitcast.15, s32[128,128]{1,0:T(8,128)} %bitcast.12, s32[1]{0:T(128)S(6)} %copy.10.row_count, s32[128,128]{1,0:T(8,128)} %bitcast.13, f32[3,128,128]{2,1,0:T(8,128)} %bitcast.10, ...), custom_call_target="tpu_custom_call" | custom-call | tf_op jit(solution)/shard_map/coupled_step/pallas_call | solution.py:518
  16.5 0.7 %copy.11 = f32[1,3,32,8,128]{4,3,2,1,0:T(8,128)} copy(f32[1,3,32,8,128]{4,3,2,1,0:T(8,128)S(1)} %bitcast.8) | data formatting | bytes 786432
